TPU v7x, 32 devices: a whole 2x2x4 slice. The times are simulated.
32 devices in a mesh: seq: 8 (over y, x, core), head: 4 (over z).
Axes of the slice: x: 2, y: 2, z: 4, core: 2. Of those that a mesh axis runs over, the one named last changes fastest.
Arguments:
- queries: bfloat16 [2048, 4096], P(('seq', 'head')), may hold values from -72 to 72
- keys: bfloat16 [2048, 2048], P(('seq', 'head')), may hold values from -6 to 6
- values: bfloat16 [2048, 2048], P(('seq', 'head')), may hold values from -6 to 6
- prefix_keys: bfloat16 [4096, 2048], P(None, 'head'), may hold values from -10 to 10
- prefix_values: bfloat16 [4096, 2048], P(None, 'head'), may hold values from -6 to 6
- span_start: int32 [1], replicated, may hold values from 0 to 4095
Outputs:
- attended: bfloat16 [2048, 4096], P(('seq', 'head'))
All inputs are finite; a program needn't handle non-finite values.
Results may differ from a plain program's by a relative error of at most 0.003.
Values may be sent and summed in bfloat16 or wider, within the bound.
No kernel may reach another device: no remote copies, remote signals or barrier semaphores. Data moves between devices by JAX's collectives and lax.ppermute only.
A program may use at most 128 MiB of HBM per device.

v0:
```python
import jax
import jax.numpy as jnp
from jax import lax
from jax.experimental import pallas as pl
from jax.experimental.pallas import tpu as pltpu
from jax.sharding import PartitionSpec as P

HEAD_DIM = 128
QH = 32
KVH = 16
QSCALE = 144
WINDOW = 4096
EXP2_SCALE = 1.4426950408889634 * QSCALE**-0.5
LOWEST = -1e30
ONES_ROWS = 16
V_ROWS = HEAD_DIM + ONES_ROWS
TILE = 512
BOTH = ("seq", "head")


def shifted(shard, axis, by):
    size = lax.axis_size(axis)
    pairs = [(i, i + by) for i in range(size) if 0 <= i + by < size]
    return lax.ppermute(shard, axis, pairs)


def shortened(shard):
    return jax.tree.map(lambda a: a.astype(jnp.bfloat16) if a.dtype == jnp.float32 else a, shard)


def attend_block(query_rows, key_rows, value_rows, query_first, key_first, start_value):
    block_rows = query_rows.shape[0]
    key_count = key_rows.shape[0]
    grouping = QH // KVH
    scaling = QSCALE ** (-0.5)
    local_groups = key_rows.shape[1] // HEAD_DIM
    query_pos = query_first + jnp.arange(block_rows, dtype=jnp.int32)
    key_pos = key_first + jnp.arange(key_count, dtype=jnp.int32)
    distance = query_pos[:, None] - key_pos[None, :]
    allowed = (distance >= 0) & (distance < WINDOW) & (start_value + key_pos >= 0)[None, :]
    outputs = []
    for key_group in range(local_groups):
        lower = key_group * grouping * HEAD_DIM
        query_head = query_rows[:, lower : lower + grouping * HEAD_DIM].reshape(
            block_rows, grouping, HEAD_DIM
        )
        key_head = key_rows[:, key_group * HEAD_DIM : (key_group + 1) * HEAD_DIM]
        value_head = value_rows[:, key_group * HEAD_DIM : (key_group + 1) * HEAD_DIM]
        scores = (
            jnp.einsum("qgd,kd->gqk", query_head, key_head, preferred_element_type=jnp.float32)
            * scaling
        )
        scores = jnp.where(allowed[None], scores, -jnp.inf)
        peak_score = jnp.max(scores, axis=2, keepdims=True)
        unnormed = jnp.exp(scores - peak_score)
        totals = jnp.sum(unnormed, axis=2)
        weights = unnormed.astype(jnp.bfloat16)
        mixture = jnp.einsum("gqk,kd->qgd", weights, value_head, preferred_element_type=jnp.float32)
        outputs.append(
            (mixture / jnp.transpose(totals)[:, :, None]).reshape(block_rows, grouping * HEAD_DIM)
        )
    return jnp.concatenate(outputs, axis=1).astype(jnp.bfloat16)


def relayed_shards(queries, keys, values, prefix_keys, prefix_values, span_start):
    query_local, key_local, value_local = (
        lax.all_to_all(queries, "head", split_axis=1, concat_axis=0, tiled=True),
        lax.all_to_all(keys, "head", split_axis=1, concat_axis=0, tiled=True),
        lax.all_to_all(values, "head", split_axis=1, concat_axis=0, tiled=True),
    )
    seq_rows = query_local.shape[0]
    shards_back = WINDOW // seq_rows
    seq_index = lax.axis_index("seq")

    def relay(step, carried):
        moving_keys, moving_values, window_keys, window_values = carried
        moving_keys, moving_values = shifted((moving_keys, moving_values), "seq", 1)
        offset = (shards_back - 1 - step) * seq_rows
        window_keys = lax.dynamic_update_slice_in_dim(window_keys, moving_keys, offset, 0)
        window_values = lax.dynamic_update_slice_in_dim(window_values, moving_values, offset, 0)
        return (moving_keys, moving_values, window_keys, window_values)

    empty = jnp.zeros((WINDOW, key_local.shape[1]), jnp.bfloat16)
    carried = lax.fori_loop(0, shards_back, relay, (key_local, value_local, empty, empty))
    window_keys = carried[2]
    window_values = carried[3]
    first_row = jnp.minimum(seq_index * seq_rows, WINDOW)
    padded_keys = jnp.concatenate([prefix_keys, jnp.zeros_like(prefix_keys)], axis=0)
    padded_values = jnp.concatenate([prefix_values, jnp.zeros_like(prefix_values)], axis=0)
    window_keys = window_keys + lax.dynamic_slice_in_dim(padded_keys, first_row, WINDOW, 0)
    window_values = window_values + lax.dynamic_slice_in_dim(padded_values, first_row, WINDOW, 0)
    all_keys = jnp.concatenate([window_keys, key_local], axis=0)
    all_values = jnp.concatenate([window_values, value_local], axis=0)
    block_rows = min(512, seq_rows)
    block_count = seq_rows // block_rows
    start_value = span_start[0]
    key_base = (seq_index - shards_back) * seq_rows
    query_base = seq_index * seq_rows

    def one_block(block_index):
        first = block_index * block_rows
        return attend_block(
            query_local, all_keys, all_values, query_base + first, key_base + first, start_value
        )

    blocks = lax.map(one_block, jnp.arange(block_count, dtype=jnp.int32))
    attended = blocks.reshape(seq_rows, query_local.shape[1])
    return lax.all_to_all(
        shortened(attended), "head", split_axis=0, concat_axis=1, tiled=True
    ).astype(attended.dtype)


def in_vmem():
    return pl.BlockSpec(memory_space=pltpu.VMEM)


def in_smem():
    return pl.BlockSpec(memory_space=pltpu.SMEM)


def in_hbm():
    return pl.BlockSpec(memory_space=pltpu.HBM)


def params(mib=32):
    return pltpu.CompilerParams(vmem_limit_bytes=mib * 2**20)


def cost(flops, moved):
    return pl.CostEstimate(flops=flops, bytes_accessed=moved, transcendentals=flops // 512)


def columns_of(head):
    return slice(head * HEAD_DIM, (head + 1) * HEAD_DIM)


def pack_heads(queries, keys, values, seq_size, head_size):
    rows = queries.shape[0]
    pairs = seq_size // 2

    def kernel(q_hbm, k_hbm, v_hbm, out_ref, q_ref, k_ref, v_ref, sems):
        copies = [
            pltpu.make_async_copy(source, target, sems.at[n])
            for n, (source, target) in enumerate(((q_hbm, q_ref), (k_hbm, k_ref), (v_hbm, v_ref)))
        ]
        for copy in copies:
            copy.start()
        copies[0].wait()
        for s in range(seq_size):
            for h in range(head_size):
                out_ref[s * head_size + h, :, :HEAD_DIM] = q_ref[:, columns_of(h * seq_size + s)]
        for parity, ref in ((0, k_ref), (1, v_ref)):
            copies[1 + parity].wait()
            for s in range(parity, seq_size, 2):
                for h in range(head_size):
                    out_ref[s * head_size + h, :, HEAD_DIM:] = ref[:, columns_of(h * pairs + s // 2)]

    return pl.pallas_call(
        kernel,
        out_shape=jax.ShapeDtypeStruct((seq_size * head_size, rows, 2 * HEAD_DIM), jnp.bfloat16),
        in_specs=[in_hbm()] * 3,
        out_specs=in_vmem(),
        scratch_shapes=[
            pltpu.VMEM(queries.shape, jnp.bfloat16),
            pltpu.VMEM(keys.shape, jnp.bfloat16),
            pltpu.VMEM(values.shape, jnp.bfloat16),
            pltpu.SemaphoreType.DMA((3,)),
        ],
        compiler_params=params(62),
        cost_estimate=cost(0, 2**21),
        name="pack_heads",
    )(queries, keys, values)


def unpack_heads(chunks, seq_size, head_size):
    rows = chunks.shape[1]

    def kernel(in_ref, out_hbm, sems):
        copies = []
        for s in range(seq_size):
            for h in range(head_size):
                n = s * head_size + h
                copies.append(
                    pltpu.make_async_copy(
                        in_ref.at[n], out_hbm.at[:, columns_of(h * seq_size + s)], sems.at[n]
                    )
                )
        for copy in copies:
            copy.start()
        for copy in copies:
            copy.wait()

    return pl.pallas_call(
        kernel,
        out_shape=jax.ShapeDtypeStruct((rows, chunks.shape[0] * HEAD_DIM), jnp.bfloat16),
        in_specs=[in_vmem()],
        out_specs=in_hbm(),
        scratch_shapes=[pltpu.SemaphoreType.DMA((chunks.shape[0],))],
        compiler_params=params(),
        name="unpack_heads",
    )(chunks)


def prefix_of_head(prefix_keys, prefix_values):
    window = prefix_keys.shape[0]
    part = window // 4

    def kernel(k_hbm, v_hbm, k_ref, v_ref, held, sems):
        at = pl.ds(pl.multiple_of(lax.axis_index("seq") // 2 * HEAD_DIM, HEAD_DIM), HEAD_DIM)
        copies = [
            pltpu.make_async_copy(
                v_hbm.at[pl.ds(n * part, part), at], held.at[pl.ds(n * part, part)], sems.at[n]
            )
            for n in range(4)
        ]
        copies.append(pltpu.make_async_copy(k_hbm.at[:, at], k_ref, sems.at[4]))
        for copy in copies:
            copy.start()
        v_ref[HEAD_DIM:, :] = jnp.ones((ONES_ROWS, window), jnp.bfloat16)
        for n in range(4):
            copies[n].wait()
            v_ref[:HEAD_DIM, n * part : (n + 1) * part] = held[n * part : (n + 1) * part, :].T
        copies[4].wait()

    return pl.pallas_call(
        kernel,
        out_shape=[
            jax.ShapeDtypeStruct((window, HEAD_DIM), jnp.bfloat16),
            jax.ShapeDtypeStruct((V_ROWS, window), jnp.bfloat16),
        ],
        in_specs=[in_hbm()] * 2,
        out_specs=[in_vmem()] * 2,
        scratch_shapes=[
            pltpu.VMEM((window, HEAD_DIM), jnp.bfloat16),
            pltpu.SemaphoreType.DMA((5,)),
        ],
        compiler_params=params(32),
        cost_estimate=cost(0, 2**23),
        name="prefix_of_head",
    )(prefix_keys, prefix_values)


def dot_turned(keys, queries):
    return lax.dot_general(
        keys, queries, (((1,), (1,)), ((), ())), preferred_element_type=jnp.float32
    )


def score_tile(keys, queries, allowed, s_ref, peak_ref):
    scores = dot_turned(keys, queries)
    if allowed is not None:
        scores = jnp.where(allowed, scores, -jnp.inf)
    s_ref[...] = scores
    return jnp.max(scores.reshape(scores.shape[0] // 8, 8, scores.shape[1]), axis=0)


def weigh_tile(s_ref, peak_ref, values, b, m_ref, acc_ref, following):
    before = m_ref[b, :1, :]
    peak = jnp.maximum(jnp.max(peak_ref[...], axis=0, keepdims=True), before)
    scaled = peak * EXP2_SCALE
    following_peak = following()
    weights = jnp.exp2(s_ref[...] * EXP2_SCALE - scaled).astype(jnp.bfloat16)
    sums = jnp.dot(values, weights, preferred_element_type=jnp.float32)
    if following_peak is not None:
        peak_ref[...] = following_peak
    acc_ref[b] = sums + acc_ref[b] * jnp.exp2(before * EXP2_SCALE - scaled)
    m_ref[b] = jnp.broadcast_to(peak, m_ref.shape[1:])


def attend_prefix(span_start, got, prefix_keys, prefix_values):
    tokens, window = got.shape[0], prefix_keys.shape[0]
    blocks = tokens // TILE

    def kernel(start_ref, q_ref, k_ref, v_ref, m_ref, acc_ref, s_a, s_b, peak_ref):
        first_key = window - start_ref[0]
        m_ref[...] = jnp.full(m_ref.shape, LOWEST, jnp.float32)
        acc_ref[...] = jnp.zeros(acc_ref.shape, jnp.float32)
        opening = [
            jnp.minimum(jnp.maximum(b * TILE + 1, first_key) // TILE, window // TILE - 1)
            for b in range(blocks)
        ]
        ends = []
        for b in range(blocks):
            count = window // TILE - 1 - opening[b]
            ends.append(count if b == 0 else ends[-1] + count)

        def place(i):
            b = sum((i >= end).astype(jnp.int32) for end in ends)
            tile = jnp.int32(0)
            for n in range(blocks):
                start = 0 if n == 0 else ends[n - 1]
                tile = jnp.where(b == n, opening[n] + 1 + i - start, tile)
            return b, pl.multiple_of(tile * TILE, TILE)

        def score(b, row, s_ref, allowed=None):
            at = pl.ds(pl.multiple_of(jnp.minimum(b, blocks - 1) * TILE, TILE), TILE)
            return score_tile(
                k_ref[pl.ds(row, TILE), :], q_ref[at, :HEAD_DIM], allowed, s_ref, peak_ref
            )

        def score_opening(b, s_ref):
            row = pl.multiple_of(opening[b] * TILE, TILE)
            key = lax.broadcasted_iota(jnp.int32, (TILE, TILE), 0)
            query = lax.broadcasted_iota(jnp.int32, (1, TILE), 1) + b * TILE
            allowed = key >= jnp.maximum(query + 1, first_key) - row
            return score(b, row, s_ref, allowed)

        def weigh(b, row, s_ref, following):
            weigh_tile(
                s_ref, peak_ref, v_ref[:, pl.ds(row, TILE)], b, m_ref, acc_ref, following
            )

        bufs = (s_a, s_b)
        peak_ref[...] = score_opening(0, s_a)
        for b in range(blocks):
            now, later = bufs[b % 2], bufs[(b + 1) % 2]
            if b + 1 < blocks:
                following = lambda b=b, later=later: score_opening(b + 1, later)
            else:
                following = lambda later=later: score(*place(jnp.int32(0)), later)
            weigh(b, pl.multiple_of(opening[b] * TILE, TILE), now, following)
        now, later = bufs[blocks % 2], bufs[(blocks + 1) % 2]

        def two(i, _):
            weigh(*place(2 * i), now, lambda: score(*place(2 * i + 1), later))
            weigh(*place(2 * i + 1), later, lambda: score(*place(2 * i + 2), now))
            return 0

        lax.fori_loop(0, (ends[-1] + 1) // 2, two, 0)

    return pl.pallas_call(
        kernel,
        out_shape=[
            jax.ShapeDtypeStruct((blocks + 1, 8, TILE), jnp.float32),
            jax.ShapeDtypeStruct((blocks + 1, V_ROWS, TILE), jnp.float32),
        ],
        in_specs=[in_smem()] + [in_vmem()] * 3,
        out_specs=[in_vmem()] * 2,
        scratch_shapes=[
            pltpu.VMEM((TILE, TILE), jnp.float32),
            pltpu.VMEM((TILE, TILE), jnp.float32),
            pltpu.VMEM((8, TILE), jnp.float32),
        ],
        compiler_params=params(),
        cost_estimate=cost(4 * tokens * window * HEAD_DIM, 2**22),
        name="attend_prefix",
    )(span_start, got, prefix_keys, prefix_values)


def attend_span(got, other, m, acc):
    tokens = got.shape[0]
    blocks = tokens // TILE

    def kernel(got_ref, other_ref, m_in, acc_in, o_ref, m_ref, acc_ref, k_ref, v_ref, s_a, s_b, peak_ref):
        holds_values = lax.axis_index("seq") % 2
        v_ref[HEAD_DIM:, :] = jnp.ones((ONES_ROWS, tokens), jnp.bfloat16)

        @pl.when(holds_values == 0)
        def _():
            k_ref[...] = got_ref[:, HEAD_DIM:]
            v_ref[:HEAD_DIM, :] = other_ref[...].T

        @pl.when(holds_values == 1)
        def _():
            k_ref[...] = other_ref[...]
            v_ref[:HEAD_DIM, :] = got_ref[:, HEAD_DIM:].T

        m_ref[...] = m_in[...]
        acc_ref[...] = acc_in[...]
        tiles = [(b, b) for b in range(blocks)]
        tiles += [(b, j) for b in range(blocks) for j in range(b)]

        def score(n, s_ref):
            b, j = tiles[n]
            allowed = None
            if b == j:
                key = lax.broadcasted_iota(jnp.int32, (TILE, TILE), 0)
                query = lax.broadcasted_iota(jnp.int32, (TILE, TILE), 1)
                allowed = key <= query
            return score_tile(
                k_ref[j * TILE : (j + 1) * TILE, :],
                got_ref[b * TILE : (b + 1) * TILE, :HEAD_DIM],
                allowed,
                s_ref,
                peak_ref,
            )

        bufs = (s_a, s_b)
        peak_ref[...] = score(0, s_a)
        for n, (b, j) in enumerate(tiles):
            more = n + 1 < len(tiles)
            weigh_tile(
                bufs[n % 2],
                peak_ref,
                v_ref[:, j * TILE : (j + 1) * TILE],
                b,
                m_ref,
                acc_ref,
                lambda n=n, more=more: score(n + 1, bufs[(n + 1) % 2]) if more else None,
            )
        for b in range(blocks):
            mixed = acc_ref[b, :HEAD_DIM, :] / acc_ref[b, HEAD_DIM : HEAD_DIM + 1, :]
            o_ref[b * TILE : (b + 1) * TILE, :] = mixed.T.astype(jnp.bfloat16)

    return pl.pallas_call(
        kernel,
        out_shape=jax.ShapeDtypeStruct((tokens, HEAD_DIM), jnp.bfloat16),
        in_specs=[in_vmem()] * 4,
        out_specs=in_vmem(),
        scratch_shapes=[
            pltpu.VMEM(m.shape, jnp.float32),
            pltpu.VMEM(acc.shape, jnp.float32),
            pltpu.VMEM((tokens, HEAD_DIM), jnp.bfloat16),
            pltpu.VMEM((V_ROWS, tokens), jnp.bfloat16),
            pltpu.VMEM((TILE, TILE), jnp.float32),
            pltpu.VMEM((TILE, TILE), jnp.float32),
            pltpu.VMEM((8, TILE), jnp.float32),
        ],
        compiler_params=params(),
        cost_estimate=cost(2 * tokens * tokens * HEAD_DIM, 2**22),
        name="attend_span",
    )(got, other, m, acc)


def spread_shards(queries, keys, values, prefix_keys, prefix_values, span_start):
    rows = queries.shape[0]
    seq_size, head_size = lax.axis_size("seq"), lax.axis_size("head")
    tokens = seq_size * head_size * rows
    packed = pack_heads(queries, keys, values, seq_size, head_size)
    got = lax.all_to_all(packed, BOTH, split_axis=0, concat_axis=0, tiled=True)
    got = got.reshape(tokens, 2 * HEAD_DIM)
    head_keys, head_values = prefix_of_head(prefix_keys, prefix_values)
    got, head_keys, head_values = lax.optimization_barrier((got, head_keys, head_values))
    other = lax.ppermute(got[:, HEAD_DIM:], "seq", [(i, i ^ 1) for i in range(seq_size)])
    m, acc = attend_prefix(span_start, got, head_keys, head_values)
    attended = attend_span(got, other, m, acc)
    attended = attended.reshape(seq_size * head_size, rows, HEAD_DIM)
    back = lax.all_to_all(attended, BOTH, split_axis=0, concat_axis=0, tiled=True)
    return unpack_heads(back, seq_size, head_size)


def solution(mesh):
    placed = (
        P(("seq", "head"), None),
        P(("seq", "head"), None),
        P(("seq", "head"), None),
        P(None, "head"),
        P(None, "head"),
        P(),
    )
    fits = mesh.shape["seq"] * mesh.shape["head"] == QH and QH == 2 * KVH
    shards = spread_shards if fits else relayed_shards
    return jax.shard_map(
        shards, mesh=mesh, in_specs=placed, out_specs=P(("seq", "head"), None), check_vma=False
    )
```

profile of v0, /device:TPU:1, one launch (start us, length us, event | category | flops | bytes accessed | tf_op | source)
XLA Modules:
  0.0 62.7 jit_solution(7380632503776427597)
XLA Ops:
  0.0 2.2 %pack_heads.1 = bf16[32,64,256]{2,1,0:T(8,128)(2,1)} custom-call(bf16[64,4096]{1,0:T(8,128)(2,1)} %q_hbm.1, bf16[64,2048]{1,0:T(8,128)(2,1)} %k_hbm.2, bf16[64,2048]{1,0:T(8,128)(2,1)} %v_hbm.2), custom_call_target="tpu_custom_call" | custom-call | bytes 2097152 | tf_op jit(solution)/shard_map/pack_heads/pallas_call | solution.py:158
  2.2 7.1 %all-to-all-start = ((bf16[32,64,256]{2,1,0:T(8,128)(2,1)}), bf16[32,64,256]{2,1,0:T(8,128)(2,1)S(1)}, u32[]{:S(2)}, u32[]{:S(2)}) async-start(bf16[32,64,256]{2,1,0:T(8,128)(2,1)} %pack_heads.1), calls=%async_computation | async-start | bytes 2097152 | tf_op jit(solution)/shard_map/all_to_all | solution.py:430
  9.3 0.0 copy-start
  9.4 2.2 %copy-done = bf16[4096,512]{1,0:T(8,128)(2,1)S(1)} copy-done((bf16[4096,512]{1,0:T(8,128)(2,1)S(1)}, bf16[4096,512]{1,0:T(8,128)(2,1)}, u32[]{:S(2)}) %copy-start) | copy-done | bytes 4194328
  11.5 0.0 copy-start.1
  11.5 2.2 %copy-done.1 = bf16[4096,512]{1,0:T(8,128)(2,1)S(1)} copy-done((bf16[4096,512]{1,0:T(8,128)(2,1)S(1)}, bf16[4096,512]{1,0:T(8,128)(2,1)}, u32[]{:S(2)}) %copy-start.1) | copy-done | bytes 4194328
  13.7 0.9 %prefix_of_head.1 = (bf16[4096,128]{1,0:T(8,128)(2,1)S(1)}, bf16[144,4096]{1,0:T(8,128)(2,1)S(1)}) custom-call(bf16[4096,512]{1,0:T(8,128)(2,1)S(1)} %copy-done, bf16[4096,512]{1,0:T(8,128)(2,1)S(1)} %copy-done.1), custom_call_target="tpu_custom_call" | custom-call | bytes 8388608 | tf_op jit(solution)/shard_map/prefix_of_head/pallas_call | solution.py:225
  14.6 21.1 %all-to-all-done = bf16[32,64,256]{2,1,0:T(8,128)(2,1)S(1)} async-done(((bf16[32,64,256]{2,1,0:T(8,128)(2,1)}), bf16[32,64,256]{2,1,0:T(8,128)(2,1)S(1)}, u32[]{:S(2)}, u32[]{:S(2)}) %all-to-all-start) | async-done | bytes 1048608 | tf_op jit(solution)/shard_map/all_to_all | solution.py:430
  35.7 0.1 collective-permute-start
  36.5 2.9 %attend_prefix.1 = (f32[5,8,512]{2,1,0:T(8,128)S(1)}, f32[5,144,512]{2,1,0:T(8,128)S(1)}) custom-call(s32[1]{0:T(128)S(6)} %copy.7.start_ref, bf16[2048,256]{1,0:T(8,128)(2,1)S(1)} %bitcast.3, bf16[4096,128]{1,0:T(8,128)(2,1)S(1)} %get-tuple-element.15.k_ref, bf16[144,4096]{1,0:T(8,128)(2,1)S(1)} %get-tuple-element.16.v_ref), custom_call_target="tpu_custom_call" | custom-call | flops 4294967296 | bytes 4194304 | tf_op jit(solution)/shard_map/attend_prefix/pallas_call | solution.py:331
  39.4 0.0 collective-permute-done.other_ref
  39.4 3.9 %attend_span.1 = bf16[2048,128]{1,0:T(8,128)(2,1)S(1)} custom-call(bf16[2048,256]{1,0:T(8,128)(2,1)S(1)} %bitcast.4, bf16[2048,128]{1,0:T(8,128)(2,1)S(1)} %collective-permute-done.other_ref, f32[5,8,512]{2,1,0:T(8,128)S(1)} %get-tuple-element.17.m_in, f32[5,144,512]{2,1,0:T(8,128)S(1)} %get-tuple-element.18.acc_in), custom_call_target="tpu_custom_call" | custom-call | flops 1073741824 | bytes 4194304 | tf_op jit(solution)/shard_map/attend_span/pallas_call | solution.py:405
  43.3 18.4 %all_to_all.10.in_ref = bf16[32,64,128]{2,1,0:T(8,128)(2,1)S(1)} all-to-all(bf16[32,64,128]{2,1,0:T(8,128)(2,1)S(1)} %bitcast.5), channel_id=1, replica_groups=mesh['seq'=8,'head'=4] {'seq','head'}, dimensions={0} | all-to-all | bytes 1048576 | tf_op jit(solution)/shard_map/all_to_all | solution.py:438
  61.7 1.1 %unpack_heads.1 = bf16[64,4096]{1,0:T(8,128)(2,1)} custom-call(bf16[32,64,128]{2,1,0:T(8,128)(2,1)S(1)} %all_to_all.10.in_ref), custom_call_target="tpu_custom_call" | custom-call | tf_op jit(solution)/shard_map/unpack_heads/pallas_call | solution.py:193
  (1 shorter events, 0.0 us)
Async XLA Ops:
  2.2 33.5 %all-to-all-start = ((bf16[32,64,256]{2,1,0:T(8,128)(2,1)}), bf16[32,64,256]{2,1,0:T(8,128)(2,1)S(1)}, u32[]{:S(2)}, u32[]{:S(2)}) async-start(bf16[32,64,256]{2,1,0:T(8,128)(2,1)} %pack_heads.1), calls=%async_computation | async-start | bytes 2097152 | tf_op jit(solution)/shard_map/all_to_all | solution.py:430
  9.3 2.2 %copy-start = (bf16[4096,512]{1,0:T(8,128)(2,1)S(1)}, bf16[4096,512]{1,0:T(8,128)(2,1)}, u32[]{:S(2)}) copy-start(bf16[4096,512]{1,0:T(8,128)(2,1)} %k_hbm.3) | copy-start | bytes 12582916
  11.5 2.2 %copy-start.1 = (bf16[4096,512]{1,0:T(8,128)(2,1)S(1)}, bf16[4096,512]{1,0:T(8,128)(2,1)}, u32[]{:S(2)}) copy-start(bf16[4096,512]{1,0:T(8,128)(2,1)} %v_hbm.3) | copy-start | bytes 12582916
  35.7 3.7 %collective-permute-start = (bf16[2048,128]{1,0:T(8,128)(2,1)S(1)}, bf16[2048,128]{1,0:T(8,128)(2,1)S(1)}, u32[]{:S(2)}, u32[]{:S(2)}) collective-permute-start(bf16[2048,128]{1,0:T(8,128)(2,1)S(1)} %slice.3), channel_id=1, source_target_pairs={{0,4},{4,0},{8,12},{12,8},{16,20},{20,16},{24,28},{28,24},{1,5},{5... | collective-permute-start | bytes 1572872 | tf_op jit(solution)/shard_map/ppermute | solution.py:434
where the time goes:
time: 63.7 us; the launch traced here: 62.7 us
  waiting for transfers between devices  21.1 us (33%)
  blocking collectives  18.4 us (29%)
  Pallas kernels  11 us (17%)
  starting transfers between devices  7.17 us (11%)
  local copies, waits for them, and re-layouts  4.41 us (7%)
  between operations  0.72 us (1%)
    all_to_all x1, waiting for transfers between devices, spread_shards(): got = lax.all_to_all(packed, BOTH, split_axis=0, concat_axis=0, tiled=True)  21.1 us
    all_to_all x1, blocking collectives, spread_shards(): lax.all_to_all(attended, BOTH, split_axis=0, concat_axis=0, tiled=True)  18.4 us
    all_to_all x1, starting transfers between devices, spread_shards(): got = lax.all_to_all(packed, BOTH, split_axis=0, concat_axis=0, tiled=True)  7.1 us
    unnamed x4, local copies, waits for them, and re-layouts  4.37 us
    pallas_call x1, Pallas kernels, attend_span(): pl.pallas_call(kernel, out_shape=jax.ShapeDtypeStruct((tokens, HEAD_DIM),...  3.89 us
    pallas_call x1, Pallas kernels, attend_prefix(): pl.pallas_call(kernel, out_shape=[jax.ShapeDtypeStruct((blocks + 1, 8, TI...  2.94 us
    pallas_call x1, Pallas kernels, pack_heads(): pl.pallas_call(kernel, out_shape=jax.ShapeDtypeStruct((seq_size * head_si...  2.23 us
  transfers between devices with their start and end apart: 2, of which 1 were waited for; matrix products, arithmetic and copies ran while one was open for 0% of the time, Pallas kernels for 6%

commit v1 on v0

--- a/solution.py
+++ b/solution.py
@@ -15,6 +15,7 @@
 ONES_ROWS = 16
 V_ROWS = HEAD_DIM + ONES_ROWS
 TILE = 512
+UNROLL = 6
 BOTH = ("seq", "head")
 
 
@@ -254,8 +255,9 @@
     return jnp.max(scores.reshape(scores.shape[0] // 8, 8, scores.shape[1]), axis=0)
 
 
-def weigh_tile(s_ref, peak_ref, values, b, m_ref, acc_ref, following):
-    before = m_ref[b, :1, :]
+def weigh_tile(s_ref, peak_ref, values, b, old, m_ref, acc_ref, following):
+    old_m, old_acc = old
+    before = old_m[b, :1, :]
     peak = jnp.maximum(jnp.max(peak_ref[...], axis=0, keepdims=True), before)
     scaled = peak * EXP2_SCALE
     following_peak = following()
@@ -263,7 +265,7 @@
     sums = jnp.dot(values, weights, preferred_element_type=jnp.float32)
     if following_peak is not None:
         peak_ref[...] = following_peak
-    acc_ref[b] = sums + acc_ref[b] * jnp.exp2(before * EXP2_SCALE - scaled)
+    acc_ref[b] = sums + old_acc[b] * jnp.exp2(before * EXP2_SCALE - scaled)
     m_ref[b] = jnp.broadcast_to(peak, m_ref.shape[1:])
 
 
@@ -307,7 +309,14 @@
 
         def weigh(b, row, s_ref, following):
             weigh_tile(
-                s_ref, peak_ref, v_ref[:, pl.ds(row, TILE)], b, m_ref, acc_ref, following
+                s_ref,
+                peak_ref,
+                v_ref[:, pl.ds(row, TILE)],
+                b,
+                (m_ref, acc_ref),
+                m_ref,
+                acc_ref,
+                following,
             )
 
         bufs = (s_a, s_b)
@@ -321,12 +330,24 @@
             weigh(b, pl.multiple_of(opening[b] * TILE, TILE), now, following)
         now, later = bufs[blocks % 2], bufs[(blocks + 1) % 2]
 
-        def two(i, _):
-            weigh(*place(2 * i), now, lambda: score(*place(2 * i + 1), later))
-            weigh(*place(2 * i + 1), later, lambda: score(*place(2 * i + 2), now))
+        def several(first, count):
+            for n in range(0, count, 2):
+                i = first + n
+                weigh(*place(i), now, lambda i=i: score(*place(i + 1), later))
+                weigh(*place(i + 1), later, lambda i=i: score(*place(i + 2), now))
+
+        many = ends[-1] // UNROLL
+
+        def unrolled(i, _):
+            several(i * UNROLL, UNROLL)
             return 0
 
-        lax.fori_loop(0, (ends[-1] + 1) // 2, two, 0)
+        def rest(i, _):
+            several(many * UNROLL + 2 * i, 2)
+            return 0
+
+        lax.fori_loop(0, many, unrolled, 0)
+        lax.fori_loop(0, (ends[-1] - many * UNROLL + 1) // 2, rest, 0)
 
     return pl.pallas_call(
         kernel,
@@ -351,22 +372,20 @@
     tokens = got.shape[0]
     blocks = tokens // TILE
 
-    def kernel(got_ref, other_ref, m_in, acc_in, o_ref, m_ref, acc_ref, k_ref, v_ref, s_a, s_b, peak_ref):
+    def kernel(got_ref, other_ref, m_in, acc_in, o_ref, m_ref, acc_ref, k_ref, v_ref, held, s_a, s_b, peak_ref):
         holds_values = lax.axis_index("seq") % 2
         v_ref[HEAD_DIM:, :] = jnp.ones((ONES_ROWS, tokens), jnp.bfloat16)
 
         @pl.when(holds_values == 0)
         def _():
             k_ref[...] = got_ref[:, HEAD_DIM:]
-            v_ref[:HEAD_DIM, :] = other_ref[...].T
+            held[...] = other_ref[...]
 
         @pl.when(holds_values == 1)
         def _():
             k_ref[...] = other_ref[...]
-            v_ref[:HEAD_DIM, :] = got_ref[:, HEAD_DIM:].T
-
-        m_ref[...] = m_in[...]
-        acc_ref[...] = acc_in[...]
+            held[...] = got_ref[:, HEAD_DIM:]
+
         tiles = [(b, b) for b in range(blocks)]
         tiles += [(b, j) for b in range(blocks) for j in range(b)]
 
@@ -389,11 +408,15 @@
         peak_ref[...] = score(0, s_a)
         for n, (b, j) in enumerate(tiles):
             more = n + 1 < len(tiles)
+            at = slice(j * TILE, (j + 1) * TILE)
+            if b == j:
+                v_ref[:HEAD_DIM, at] = held[at, :].T
             weigh_tile(
                 bufs[n % 2],
                 peak_ref,
                 v_ref[:, j * TILE : (j + 1) * TILE],
                 b,
+                (m_in, acc_in) if b == j else (m_ref, acc_ref),
                 m_ref,
                 acc_ref,
                 lambda n=n, more=more: score(n + 1, bufs[(n + 1) % 2]) if more else None,
@@ -412,6 +435,7 @@
             pltpu.VMEM(acc.shape, jnp.float32),
             pltpu.VMEM((tokens, HEAD_DIM), jnp.bfloat16),
             pltpu.VMEM((V_ROWS, tokens), jnp.bfloat16),
+            pltpu.VMEM((tokens, HEAD_DIM), jnp.bfloat16),
             pltpu.VMEM((TILE, TILE), jnp.float32),
             pltpu.VMEM((TILE, TILE), jnp.float32),
             pltpu.VMEM((8, TILE), jnp.float32),

time: 63.7 us -> 65.9 us (1.035)
  Pallas kernels: 11 us -> 13.2 us
    pallas_call x1, Pallas kernels: 2.94 us -> 5.18 us  [attend_prefix(): pl.pallas_call(kernel, out_shape=[jax.ShapeDtypeStruct((blocks + 1, 8, TI...]
  transfers between devices with their start and end apart: 2 -> 2, of which waited for: 1 -> 1; matrix products, arithmetic and copies ran while one was open for 0% -> 0% of each run, Pallas kernels for 6% -> 9%
where the time goes in v1:
time: 65.9 us; the launch traced here: 64.9 us
  waiting for transfers between devices  21.1 us (32%)
  blocking collectives  18.4 us (28%)
  Pallas kernels  13.2 us (20%)
  starting transfers between devices  7.17 us (11%)
  local copies, waits for them, and re-layouts  4.41 us (7%)
  between operations  0.72 us (1%)
    all_to_all x1, waiting for transfers between devices, spread_shards(): got = lax.all_to_all(packed, BOTH, split_axis=0, concat_axis=0, tiled=True)  21.1 us
    all_to_all x1, blocking collectives, spread_shards(): lax.all_to_all(attended, BOTH, split_axis=0, concat_axis=0, tiled=True)  18.4 us
    all_to_all x1, starting transfers between devices, spread_shards(): got = lax.all_to_all(packed, BOTH, split_axis=0, concat_axis=0, tiled=True)  7.1 us
    pallas_call x1, Pallas kernels, attend_prefix(): pl.pallas_call(kernel, out_shape=[jax.ShapeDtypeStruct((blocks + 1, 8, TI...  5.18 us
    unnamed x4, local copies, waits for them, and re-layouts  4.37 us
    pallas_call x1, Pallas kernels, attend_span(): pl.pallas_call(kernel, out_shape=jax.ShapeDtypeStruct((tokens, HEAD_DIM),...  3.82 us
    pallas_call x1, Pallas kernels, pack_heads(): pl.pallas_call(kernel, out_shape=jax.ShapeDtypeStruct((seq_size * head_si...  2.23 us
  transfers between devices with their start and end apart: 2, of which 1 were waited for; matrix products, arithmetic and copies ran while one was open for 0% of the time, Pallas kernels for 9%

profile of v1, /device:TPU:1, one launch (start us, length us, event | category | flops | bytes accessed | tf_op | source)
XLA Modules:
  0.0 64.9 jit_solution(4595403215779813538)
XLA Ops:
  0.0 2.2 %pack_heads.1 = bf16[32,64,256]{2,1,0:T(8,128)(2,1)} custom-call(bf16[64,4096]{1,0:T(8,128)(2,1)} %q_hbm.1, bf16[64,2048]{1,0:T(8,128)(2,1)} %k_hbm.2, bf16[64,2048]{1,0:T(8,128)(2,1)} %v_hbm.2), custom_call_target="tpu_custom_call" | custom-call | bytes 2097152 | tf_op jit(solution)/shard_map/pack_heads/pallas_call | solution.py:159
  2.2 7.1 %all-to-all-start = ((bf16[32,64,256]{2,1,0:T(8,128)(2,1)}), bf16[32,64,256]{2,1,0:T(8,128)(2,1)S(1)}, u32[]{:S(2)}, u32[]{:S(2)}) async-start(bf16[32,64,256]{2,1,0:T(8,128)(2,1)} %pack_heads.1), calls=%async_computation | async-start | bytes 2097152 | tf_op jit(solution)/shard_map/all_to_all | solution.py:454
  9.3 0.0 copy-start
  9.4 2.2 %copy-done = bf16[4096,512]{1,0:T(8,128)(2,1)S(1)} copy-done((bf16[4096,512]{1,0:T(8,128)(2,1)S(1)}, bf16[4096,512]{1,0:T(8,128)(2,1)}, u32[]{:S(2)}) %copy-start) | copy-done | bytes 4194328
  11.5 0.0 copy-start.1
  11.5 2.2 %copy-done.1 = bf16[4096,512]{1,0:T(8,128)(2,1)S(1)} copy-done((bf16[4096,512]{1,0:T(8,128)(2,1)S(1)}, bf16[4096,512]{1,0:T(8,128)(2,1)}, u32[]{:S(2)}) %copy-start.1) | copy-done | bytes 4194328
  13.7 0.9 %prefix_of_head.1 = (bf16[4096,128]{1,0:T(8,128)(2,1)S(1)}, bf16[144,4096]{1,0:T(8,128)(2,1)S(1)}) custom-call(bf16[4096,512]{1,0:T(8,128)(2,1)S(1)} %copy-done, bf16[4096,512]{1,0:T(8,128)(2,1)S(1)} %copy-done.1), custom_call_target="tpu_custom_call" | custom-call | bytes 8388608 | tf_op jit(solution)/shard_map/prefix_of_head/pallas_call | solution.py:226
  14.6 21.1 %all-to-all-done = bf16[32,64,256]{2,1,0:T(8,128)(2,1)S(1)} async-done(((bf16[32,64,256]{2,1,0:T(8,128)(2,1)}), bf16[32,64,256]{2,1,0:T(8,128)(2,1)S(1)}, u32[]{:S(2)}, u32[]{:S(2)}) %all-to-all-start) | async-done | bytes 1048608 | tf_op jit(solution)/shard_map/all_to_all | solution.py:454
  35.7 0.1 collective-permute-start
  36.5 5.2 %attend_prefix.1 = (f32[5,8,512]{2,1,0:T(8,128)S(1)}, f32[5,144,512]{2,1,0:T(8,128)S(1)}) custom-call(s32[1]{0:T(128)S(6)} %copy.7.start_ref, bf16[2048,256]{1,0:T(8,128)(2,1)S(1)} %bitcast.3, bf16[4096,128]{1,0:T(8,128)(2,1)S(1)} %get-tuple-element.15.k_ref, bf16[144,4096]{1,0:T(8,128)(2,1)S(1)} %get-tuple-element.16.v_ref), custom_call_target="tpu_custom_call" | custom-call | flops 4294967296 | bytes 4194304 | tf_op jit(solution)/shard_map/attend_prefix/pallas_call | solution.py:352
  41.7 0.0 collective-permute-done.other_ref
  41.7 3.8 %attend_span.1 = bf16[2048,128]{1,0:T(8,128)(2,1)S(1)} custom-call(bf16[2048,256]{1,0:T(8,128)(2,1)S(1)} %bitcast.4, bf16[2048,128]{1,0:T(8,128)(2,1)S(1)} %collective-permute-done.other_ref, f32[5,8,512]{2,1,0:T(8,128)S(1)} %get-tuple-element.17.m_in, f32[5,144,512]{2,1,0:T(8,128)S(1)} %get-tuple-element.18.acc_in), custom_call_target="tpu_custom_call" | custom-call | flops 1073741824 | bytes 4194304 | tf_op jit(solution)/shard_map/attend_span/pallas_call | solution.py:428
  45.5 18.4 %all_to_all.10.in_ref = bf16[32,64,128]{2,1,0:T(8,128)(2,1)S(1)} all-to-all(bf16[32,64,128]{2,1,0:T(8,128)(2,1)S(1)} %bitcast.5), channel_id=1, replica_groups=mesh['seq'=8,'head'=4] {'seq','head'}, dimensions={0} | all-to-all | bytes 1048576 | tf_op jit(solution)/shard_map/all_to_all | solution.py:462
  63.9 1.1 %unpack_heads.1 = bf16[64,4096]{1,0:T(8,128)(2,1)} custom-call(bf16[32,64,128]{2,1,0:T(8,128)(2,1)S(1)} %all_to_all.10.in_ref), custom_call_target="tpu_custom_call" | custom-call | tf_op jit(solution)/shard_map/unpack_heads/pallas_call | solution.py:194
  (1 shorter events, 0.0 us)
Async XLA Ops:
  2.2 33.5 %all-to-all-start = ((bf16[32,64,256]{2,1,0:T(8,128)(2,1)}), bf16[32,64,256]{2,1,0:T(8,128)(2,1)S(1)}, u32[]{:S(2)}, u32[]{:S(2)}) async-start(bf16[32,64,256]{2,1,0:T(8,128)(2,1)} %pack_heads.1), calls=%async_computation | async-start | bytes 2097152 | tf_op jit(solution)/shard_map/all_to_all | solution.py:454
  9.3 2.2 %copy-start = (bf16[4096,512]{1,0:T(8,128)(2,1)S(1)}, bf16[4096,512]{1,0:T(8,128)(2,1)}, u32[]{:S(2)}) copy-start(bf16[4096,512]{1,0:T(8,128)(2,1)} %k_hbm.3) | copy-start | bytes 12582916
  11.5 2.2 %copy-start.1 = (bf16[4096,512]{1,0:T(8,128)(2,1)S(1)}, bf16[4096,512]{1,0:T(8,128)(2,1)}, u32[]{:S(2)}) copy-start(bf16[4096,512]{1,0:T(8,128)(2,1)} %v_hbm.3) | copy-start | bytes 12582916
  35.7 5.9 %collective-permute-start = (bf16[2048,128]{1,0:T(8,128)(2,1)S(1)}, bf16[2048,128]{1,0:T(8,128)(2,1)S(1)}, u32[]{:S(2)}, u32[]{:S(2)}) collective-permute-start(bf16[2048,128]{1,0:T(8,128)(2,1)S(1)} %slice.3), channel_id=1, source_target_pairs={{0,4},{4,0},{8,12},{12,8},{16,20},{20,16},{24,28},{28,24},{1,5},{5... | collective-permute-start | bytes 1572872 | tf_op jit(solution)/shard_map/ppermute | solution.py:458

commit v2 on v1

--- a/solution.py
+++ b/solution.py
@@ -261,8 +261,12 @@
     peak = jnp.maximum(jnp.max(peak_ref[...], axis=0, keepdims=True), before)
     scaled = peak * EXP2_SCALE
     following_peak = following()
-    weights = jnp.exp2(s_ref[...] * EXP2_SCALE - scaled).astype(jnp.bfloat16)
-    sums = jnp.dot(values, weights, preferred_element_type=jnp.float32)
+    parts = []
+    for n in range(2):
+        at = slice(n * (TILE // 2), (n + 1) * (TILE // 2))
+        weights = jnp.exp2(s_ref[:, at] * EXP2_SCALE - scaled[:, at]).astype(jnp.bfloat16)
+        parts.append(jnp.dot(values, weights, preferred_element_type=jnp.float32))
+    sums = jnp.concatenate(parts, axis=1)
     if following_peak is not None:
         peak_ref[...] = following_peak
     acc_ref[b] = sums + old_acc[b] * jnp.exp2(before * EXP2_SCALE - scaled)

time: 65.9 us -> 66.5 us (level); the launches traced: 64.9 us -> 67.4 us
  Pallas kernels: 13.2 us -> 15.7 us
    pallas_call x1, Pallas kernels: 5.18 us -> 7.7 us  [attend_prefix(): pl.pallas_call(kernel, out_shape=[jax.ShapeDtypeStruct((blocks + 1, 8, TI...]
  transfers between devices with their start and end apart: 2 -> 2, of which waited for: 1 -> 1; matrix products, arithmetic and copies ran while one was open for 0% -> 0% of each run, Pallas kernels for 9% -> 13%
where the time goes in v2:
time: 66.5 us; the launch traced here: 67.4 us
  waiting for transfers between devices  21.1 us (32%)
  blocking collectives  18.4 us (28%)
  Pallas kernels  15.7 us (24%)
  starting transfers between devices  7.17 us (11%)
  local copies, waits for them, and re-layouts  4.41 us (7%)
  between operations  0.72 us (1%)
    all_to_all x1, waiting for transfers between devices, spread_shards(): got = lax.all_to_all(packed, BOTH, split_axis=0, concat_axis=0, tiled=True)  21.1 us
    all_to_all x1, blocking collectives, spread_shards(): lax.all_to_all(attended, BOTH, split_axis=0, concat_axis=0, tiled=True)  18.4 us
    pallas_call x1, Pallas kernels, attend_prefix(): pl.pallas_call(kernel, out_shape=[jax.ShapeDtypeStruct((blocks + 1, 8, TI...  7.7 us
    all_to_all x1, starting transfers between devices, spread_shards(): got = lax.all_to_all(packed, BOTH, split_axis=0, concat_axis=0, tiled=True)  7.1 us
    unnamed x4, local copies, waits for them, and re-layouts  4.37 us
    pallas_call x1, Pallas kernels, attend_span(): pl.pallas_call(kernel, out_shape=jax.ShapeDtypeStruct((tokens, HEAD_DIM),...  3.83 us
    pallas_call x1, Pallas kernels, pack_heads(): pl.pallas_call(kernel, out_shape=jax.ShapeDtypeStruct((seq_size * head_si...  2.23 us
  transfers between devices with their start and end apart: 2, of which 1 were waited for; matrix products, arithmetic and copies ran while one was open for 0% of the time, Pallas kernels for 13%

profile of v2, /device:TPU:1, one launch (start us, length us, event | category | flops | bytes accessed | tf_op | source)
XLA Modules:
  0.0 67.4 jit_solution(8942482896523169360)
XLA Ops:
  0.0 2.2 %pack_heads.1 = bf16[32,64,256]{2,1,0:T(8,128)(2,1)} custom-call(bf16[64,4096]{1,0:T(8,128)(2,1)} %q_hbm.1, bf16[64,2048]{1,0:T(8,128)(2,1)} %k_hbm.2, bf16[64,2048]{1,0:T(8,128)(2,1)} %v_hbm.2), custom_call_target="tpu_custom_call" | custom-call | bytes 2097152 | tf_op jit(solution)/shard_map/pack_heads/pallas_call | solution.py:159
  2.2 7.1 %all-to-all-start = ((bf16[32,64,256]{2,1,0:T(8,128)(2,1)}), bf16[32,64,256]{2,1,0:T(8,128)(2,1)S(1)}, u32[]{:S(2)}, u32[]{:S(2)}) async-start(bf16[32,64,256]{2,1,0:T(8,128)(2,1)} %pack_heads.1), calls=%async_computation | async-start | bytes 2097152 | tf_op jit(solution)/shard_map/all_to_all | solution.py:458
  9.3 0.0 copy-start
  9.4 2.2 %copy-done = bf16[4096,512]{1,0:T(8,128)(2,1)S(1)} copy-done((bf16[4096,512]{1,0:T(8,128)(2,1)S(1)}, bf16[4096,512]{1,0:T(8,128)(2,1)}, u32[]{:S(2)}) %copy-start) | copy-done | bytes 4194328
  11.5 0.0 copy-start.1
  11.5 2.2 %copy-done.1 = bf16[4096,512]{1,0:T(8,128)(2,1)S(1)} copy-done((bf16[4096,512]{1,0:T(8,128)(2,1)S(1)}, bf16[4096,512]{1,0:T(8,128)(2,1)}, u32[]{:S(2)}) %copy-start.1) | copy-done | bytes 4194328
  13.7 0.9 %prefix_of_head.1 = (bf16[4096,128]{1,0:T(8,128)(2,1)S(1)}, bf16[144,4096]{1,0:T(8,128)(2,1)S(1)}) custom-call(bf16[4096,512]{1,0:T(8,128)(2,1)S(1)} %copy-done, bf16[4096,512]{1,0:T(8,128)(2,1)S(1)} %copy-done.1), custom_call_target="tpu_custom_call" | custom-call | bytes 8388608 | tf_op jit(solution)/shard_map/prefix_of_head/pallas_call | solution.py:226
  14.6 21.1 %all-to-all-done = bf16[32,64,256]{2,1,0:T(8,128)(2,1)S(1)} async-done(((bf16[32,64,256]{2,1,0:T(8,128)(2,1)}), bf16[32,64,256]{2,1,0:T(8,128)(2,1)S(1)}, u32[]{:S(2)}, u32[]{:S(2)}) %all-to-all-start) | async-done | bytes 1048608 | tf_op jit(solution)/shard_map/all_to_all | solution.py:458
  35.7 0.1 collective-permute-start
  36.5 7.7 %attend_prefix.1 = (f32[5,8,512]{2,1,0:T(8,128)S(1)}, f32[5,144,512]{2,1,0:T(8,128)S(1)}) custom-call(s32[1]{0:T(128)S(6)} %copy.7.start_ref, bf16[2048,256]{1,0:T(8,128)(2,1)S(1)} %bitcast.3, bf16[4096,128]{1,0:T(8,128)(2,1)S(1)} %get-tuple-element.15.k_ref, bf16[144,4096]{1,0:T(8,128)(2,1)S(1)} %get-tuple-element.16.v_ref), custom_call_target="tpu_custom_call" | custom-call | flops 4294967296 | bytes 4194304 | tf_op jit(solution)/shard_map/attend_prefix/pallas_call | solution.py:356
  44.2 0.0 collective-permute-done.other_ref
  44.2 3.8 %attend_span.1 = bf16[2048,128]{1,0:T(8,128)(2,1)S(1)} custom-call(bf16[2048,256]{1,0:T(8,128)(2,1)S(1)} %bitcast.4, bf16[2048,128]{1,0:T(8,128)(2,1)S(1)} %collective-permute-done.other_ref, f32[5,8,512]{2,1,0:T(8,128)S(1)} %get-tuple-element.17.m_in, f32[5,144,512]{2,1,0:T(8,128)S(1)} %get-tuple-element.18.acc_in), custom_call_target="tpu_custom_call" | custom-call | flops 1073741824 | bytes 4194304 | tf_op jit(solution)/shard_map/attend_span/pallas_call | solution.py:432
  48.0 18.4 %all_to_all.10.in_ref = bf16[32,64,128]{2,1,0:T(8,128)(2,1)S(1)} all-to-all(bf16[32,64,128]{2,1,0:T(8,128)(2,1)S(1)} %bitcast.5), channel_id=1, replica_groups=mesh['seq'=8,'head'=4] {'seq','head'}, dimensions={0} | all-to-all | bytes 1048576 | tf_op jit(solution)/shard_map/all_to_all | solution.py:466
  66.4 1.1 %unpack_heads.1 = bf16[64,4096]{1,0:T(8,128)(2,1)} custom-call(bf16[32,64,128]{2,1,0:T(8,128)(2,1)S(1)} %all_to_all.10.in_ref), custom_call_target="tpu_custom_call" | custom-call | tf_op jit(solution)/shard_map/unpack_heads/pallas_call | solution.py:194
  (1 shorter events, 0.0 us)
Async XLA Ops:
  2.2 33.5 %all-to-all-start = ((bf16[32,64,256]{2,1,0:T(8,128)(2,1)}), bf16[32,64,256]{2,1,0:T(8,128)(2,1)S(1)}, u32[]{:S(2)}, u32[]{:S(2)}) async-start(bf16[32,64,256]{2,1,0:T(8,128)(2,1)} %pack_heads.1), calls=%async_computation | async-start | bytes 2097152 | tf_op jit(solution)/shard_map/all_to_all | solution.py:458
  9.3 2.2 %copy-start = (bf16[4096,512]{1,0:T(8,128)(2,1)S(1)}, bf16[4096,512]{1,0:T(8,128)(2,1)}, u32[]{:S(2)}) copy-start(bf16[4096,512]{1,0:T(8,128)(2,1)} %k_hbm.3) | copy-start | bytes 12582916
  11.5 2.2 %copy-start.1 = (bf16[4096,512]{1,0:T(8,128)(2,1)S(1)}, bf16[4096,512]{1,0:T(8,128)(2,1)}, u32[]{:S(2)}) copy-start(bf16[4096,512]{1,0:T(8,128)(2,1)} %v_hbm.3) | copy-start | bytes 12582916
  35.7 8.4 %collective-permute-start = (bf16[2048,128]{1,0:T(8,128)(2,1)S(1)}, bf16[2048,128]{1,0:T(8,128)(2,1)S(1)}, u32[]{:S(2)}, u32[]{:S(2)}) collective-permute-start(bf16[2048,128]{1,0:T(8,128)(2,1)S(1)} %slice.3), channel_id=1, source_target_pairs={{0,4},{4,0},{8,12},{12,8},{16,20},{20,16},{24,28},{28,24},{1,5},{5... | collective-permute-start | bytes 1572872 | tf_op jit(solution)/shard_map/ppermute | solution.py:462
